TPU v7x, 512 devices: a whole 4x4x16 slice. The times are simulated.
512 devices in a mesh: pair: 16 (over y, z_lo), row: 32 (over z_hi, x, core).
Axes of the slice: x: 4, y: 4, z: 16 (z_hi: 4, z_lo: 4; z = z_hi * 4 + z_lo), core: 2. Of those that a mesh axis runs over, the one named last changes fastest.
Arguments:
- matrix: float32 [65536, 4096], P('row', 'pair'), may hold values from -500 to 500, as said below
Outputs:
- rotated: float32 [65536, 4096], P('row', 'pair')
Inputs may be any that keep to these rules, and one draw needn't show every extreme that they name: Real entries of the matrix.
All inputs are finite; a program needn't handle non-finite values.
Results may differ from a plain program's by a relative error of at most 0.0003.
Values sent between devices are 32-bit elements; how exact they have to be, the bound alone decides.
A program may use at most 64 MiB of HBM per device.

v0:
```python
import jax
import jax.numpy as jnp
from jax import lax
from jax.sharding import PartitionSpec as P

ROUNDS = 128


def passed_along(block, axis, distance):
    devices = range(lax.axis_size(axis))
    route = [(i - distance, i) for i in devices if i - distance in devices]
    return lax.ppermute(block, axis, route)


def shift_down(values, along_axis):
    size_along = values.shape[along_axis]
    head_part = lax.slice_in_dim(values, 1, size_along, axis=along_axis)
    tail_part = lax.slice_in_dim(values, 0, 1, axis=along_axis)
    return jnp.concatenate([head_part, tail_part], axis=along_axis)


def roll_static(values, offset, along_axis):
    size_along = values.shape[along_axis]
    amount = offset % size_along
    if amount == 0:
        return values
    head_part = lax.slice_in_dim(values, size_along - amount, size_along, axis=along_axis)
    tail_part = lax.slice_in_dim(values, 0, size_along - amount, axis=along_axis)
    return jnp.concatenate([head_part, tail_part], axis=along_axis)


def roll_half_down(values, along_axis):
    half_size = values.shape[along_axis] // 2
    first_half = lax.slice_in_dim(values, 0, half_size, axis=along_axis)
    second_half = lax.slice_in_dim(values, half_size, 2 * half_size, axis=along_axis)
    return jnp.concatenate([first_half, shift_down(second_half, along_axis)], axis=along_axis)


def rotate_pairs(values, cosine, sine_part, along_axis):
    half_size = values.shape[along_axis] // 2
    first_half = lax.slice_in_dim(values, 0, half_size, axis=along_axis)
    second_half = lax.slice_in_dim(values, half_size, 2 * half_size, axis=along_axis)
    if along_axis == 0:
        cosine = cosine[:, None]
        sine_part = sine_part[:, None]
    new_first = first_half * cosine - second_half * sine_part
    new_second = first_half * sine_part + second_half * cosine
    return jnp.concatenate([new_first, new_second], axis=along_axis)


def unit_mask(size_now):
    row_ids = lax.broadcasted_iota(jnp.int32, (size_now, size_now), 0)
    col_ids = lax.broadcasted_iota(jnp.int32, (size_now, size_now), 1)
    return (row_ids == col_ids).astype(jnp.float32)


def masked_diagonal(square, mask_table):
    return jnp.sum(square * mask_table, axis=1)


def jacobi_rounds(gram_pair):
    full_size = gram_pair.shape[0]
    half_size = full_size // 2
    mask_table = unit_mask(half_size)
    mixing = unit_mask(full_size)

    def one_round(round_index, carry):
        gram_now, mixing_now = carry
        alpha_norm = masked_diagonal(gram_now[:half_size, :half_size], mask_table)
        beta_norm = masked_diagonal(gram_now[half_size:, half_size:], mask_table)
        gamma_cross = masked_diagonal(gram_now[:half_size, half_size:], mask_table)
        spread = beta_norm - alpha_norm
        half_angle = 0.5 * jnp.arctan2(2.0 * gamma_cross * jnp.sign(spread), jnp.abs(spread))
        cosine = jnp.cos(half_angle)
        sine_part = jnp.sin(half_angle)
        gram_now = rotate_pairs(rotate_pairs(gram_now, cosine, sine_part, 1), cosine, sine_part, 0)
        mixing_now = rotate_pairs(mixing_now, cosine, sine_part, 1)
        gram_now = roll_half_down(roll_half_down(gram_now, 0), 1)
        mixing_now = roll_half_down(mixing_now, 1)
        return (gram_now, mixing_now)

    gram_pair, mixing = lax.fori_loop(0, ROUNDS, one_round, (gram_pair, mixing))
    first_half = mixing[:, :half_size]
    second_half = roll_static(mixing[:, half_size:], ROUNDS % half_size, 1)
    return jnp.concatenate([first_half, second_half], axis=1)


def cross_product(first_part, second_part):
    return lax.dot_general(
        first_part,
        second_part,
        (((0,), (0,)), ((), ())),
        precision=lax.Precision.HIGHEST,
        preferred_element_type=jnp.float32,
    )


def apply_mixing(first_part, second_part, columns):
    half_size = first_part.shape[1]
    upper_rows = jnp.dot(
        first_part,
        columns[:half_size],
        precision=lax.Precision.HIGHEST,
        preferred_element_type=jnp.float32,
    )
    return upper_rows + jnp.dot(
        second_part,
        columns[half_size:],
        precision=lax.Precision.HIGHEST,
        preferred_element_type=jnp.float32,
    )


def pair_gram(left_block, right_block):
    left_left = cross_product(left_block, left_block)
    left_right = cross_product(left_block, right_block)
    right_right = cross_product(right_block, right_block)
    whole_gram = jnp.block([[left_left, left_right], [left_right.T, right_right]])
    return lax.psum(whole_gram, "row")


def per_device(matrix):
    half_size = matrix.shape[1] // 2
    pair_count = lax.axis_size("pair")
    position = lax.axis_index("pair")
    keep_first = position == 0
    keep_last = position == pair_count - 1
    left_block = matrix[:, :half_size]
    right_block = matrix[:, half_size:]
    mixing = jacobi_rounds(pair_gram(left_block, right_block))
    rotated_left = apply_mixing(left_block, right_block, mixing[:, :half_size])
    rotated_right = apply_mixing(left_block, right_block, mixing[:, half_size:])
    forward_piece = jnp.where(keep_first, rotated_right, rotated_left)
    from_before = passed_along(forward_piece, "pair", 1)
    from_after = passed_along(rotated_right, "pair", -1)
    left_block = jnp.where(keep_first, rotated_left, from_before)
    right_block = jnp.where(keep_last, rotated_left, from_after)
    return jnp.concatenate([left_block, right_block], axis=1)


def solution(mesh):
    in_specs = (P("row", "pair"),)
    out_specs = P("row", "pair")
    return jax.shard_map(
        per_device, mesh=mesh, in_specs=in_specs, out_specs=out_specs, check_vma=False
    )
```

profile of v0, /device:TPU:1, one launch (start us, length us, event | category | flops | bytes accessed | tf_op | source)
XLA Modules:
  0.0 552.2 jit_solution(17905390946460803674)
XLA Ops:
  6.5 3.5 fusion.9
  10.1 1.8 fusion.7
  11.9 1.8 fusion.16
  13.8 0.7 maximum_maximum_fusion
  14.6 351.5 %all-reduce.2.cloned.1.call-done = f32[256,256]{0,1:T(8,128)} async-done(((f32[256,256]{0,1:T(8,128)}), f32[256,256]{0,1:T(8,128)}) %all-reduce.2.cloned.1.call-update) | async-done | bytes 262160 | tf_op jit(solution)/shard_map/psum | solution.py:119
  366.1 1.1 copy.3
  367.2 117.5 %while.14 = (s32[]{:T(128)}, f32[256,256]{1,0:T(8,128)S(1)}, f32[256,256]{1,0:T(8,128)S(1)}, s32[]{:T(128)}) while((s32[]{:T(128)}, f32[256,256]{1,0:T(8,128)S(1)}, f32[256,256]{1,0:T(8,128)S(1)}, s32[]{:T(128)}) %tuple.46), condition=%wide.region_5.6_spmd.clone.clone, body=%wide.region_1.5_spmd.clone.clone.sunk | while | flops 1196418 | bytes 4396085 | solution.py:82
  367.2 0.1 select_reduce_fusion.4
  368.1 0.1 select_reduce_fusion.4
  369.0 0.1 select_reduce_fusion.4
  369.9 0.1 select_reduce_fusion.4
  370.8 0.1 select_reduce_fusion.4
  374.5 0.1 select_reduce_fusion.4
  378.2 0.1 select_reduce_fusion.4
  384.6 0.1 select_reduce_fusion.4
  388.3 0.1 select_reduce_fusion.4
  391.9 0.1 select_reduce_fusion.4
  395.6 0.1 select_reduce_fusion.4
  402.0 0.1 select_reduce_fusion.4
  405.7 0.1 select_reduce_fusion.4
  409.4 0.1 select_reduce_fusion.4
  413.1 0.1 select_reduce_fusion.4
  419.5 0.1 select_reduce_fusion.4
  423.2 0.1 select_reduce_fusion.4
  426.8 0.1 select_reduce_fusion.4
  430.5 0.1 select_reduce_fusion.4
  436.9 0.1 select_reduce_fusion.4
  440.6 0.1 select_reduce_fusion.4
  444.3 0.1 select_reduce_fusion.4
  447.9 0.1 select_reduce_fusion.4
  454.4 0.1 select_reduce_fusion.4
  458.0 0.1 select_reduce_fusion.4
  461.7 0.1 select_reduce_fusion.4
  465.4 0.1 select_reduce_fusion.4
  471.8 0.1 select_reduce_fusion.4
  475.5 0.1 select_reduce_fusion.4
  479.1 0.1 select_reduce_fusion.4
  482.8 0.1 select_reduce_fusion.4
  484.6 1.1 fusion.13
  485.7 1.1 fusion.11
  486.8 1.1 fusion.4
  487.9 2.5 broadcast_select_fusion.2
  490.4 2.3 collective-permute-start
  492.8 1.3 collective-permute-start.1
  494.1 21.1 %collective-permute-done = f32[2048,128]{0,1:T(8,128)S(1)} collective-permute-done((f32[2048,128]{0,1:T(8,128)}, f32[2048,128]{0,1:T(8,128)S(1)}, u32[]{:S(2)}, u32[]{:S(2)}) %collective-permute-start) | collective-permute-done | bytes 1048608 | tf_op jit(solution)/shard_map/ppermute | solution.py:12
  515.2 26.8 %collective-permute-done.1 = f32[2048,128]{0,1:T(8,128)S(1)} collective-permute-done((f32[2048,128]{0,1:T(8,128)}, f32[2048,128]{0,1:T(8,128)S(1)}, u32[]{:S(2)}, u32[]{:S(2)}) %collective-permute-start.1) | collective-permute-done | bytes 1048608 | tf_op jit(solution)/shard_map/ppermute | solution.py:12
  542.0 1.4 broadcast_select_fusion.1
  543.6 1.8 copy.4
  (1642 shorter events, 100.2 us)
Async XLA Ops:
  6.5 3.5 copy-start
  6.5 359.5 %all-reduce.2.cloned.1.call-start = ((), (), s32[]{:S(2)}) async-start(), calls=%async_computation | async-start | bytes 524288 | tf_op jit(solution)/shard_map/psum | solution.py:119
  487.9 2.5 copy-start.1
  490.4 24.8 %collective-permute-start = (f32[2048,128]{0,1:T(8,128)}, f32[2048,128]{0,1:T(8,128)S(1)}, u32[]{:S(2)}, u32[]{:S(2)}) collective-permute-start(f32[2048,128]{0,1:T(8,128)} %get-tuple-element.81), channel_id=1, source_target_pairs={{0,32},{32,64},{64,96},{96,128},{128,160},{160,192},{192,224},{224... | collective-permute-start | bytes 3145736 | tf_op jit(solution)/shard_map/ppermute | solution.py:12
  492.8 49.2 %collective-permute-start.1 = (f32[2048,128]{0,1:T(8,128)}, f32[2048,128]{0,1:T(8,128)S(1)}, u32[]{:S(2)}, u32[]{:S(2)}) collective-permute-start(f32[2048,128]{0,1:T(8,128)} %get-tuple-element.82), channel_id=1, source_target_pairs={{32,0},{64,32},{96,64},{128,96},{160,128},{192,160},{224,192},{256... | collective-permute-start | bytes 3145736 | tf_op jit(solution)/shard_map/ppermute | solution.py:12
Sparse Core Ops, SparseCore 0:
  14.7 351.3 all-reduce.1
where the time goes:
time: 552 us
  waiting for transfers between devices  399 us (72%)
  other arithmetic  73.7 us (13%)
  local copies, waits for them, and re-layouts  36 us (7%)
  between operations  13.5 us (2%)
  loops' own time  13.1 us (2%)
  matrix products  12.9 us (2%)
    psum x1, waiting for transfers between devices, pair_gram(): return lax.psum(whole_gram, 'row')  351 us
    ppermute x2, waiting for transfers between devices, passed_along(): return lax.ppermute(block, axis, route)  47.9 us
    slice x384, local copies, waits for them, and re-layouts, shift_down(): head_part = lax.slice_in_dim(values, 1, size_along, axis=along_axis)  24.7 us
    sub x256, other arithmetic, rotate_pairs(): new_first = first_half * cosine - second_half * sine_part  21 us
    concatenate x256, other arithmetic, roll_half_down(): jnp.concatenate([first_half, shift_down(second_half, along_axis)], axis=a...  20.8 us
    reduce_sum x128, other arithmetic, masked_diagonal(): return jnp.sum(square * mask_table, axis=1)  18.4 us
    another operation x1, loops' own time, jacobi_rounds(): gram_pair, mixing = lax.fori_loop(0, ROUNDS, one_round, (gram_pair, mixing))  13.1 us
    cos x128, other arithmetic, one_round(): cosine = jnp.cos(half_angle)  11.2 us
  transfers between devices with their start and end apart: 3, of which 3 were waited for; matrix products, arithmetic and copies ran while one was open for 0% of the time, Pallas kernels for 0%

commit v1 on v0

v1 whole, which is shorter than its diff:
```python
import functools

import jax
import jax.numpy as jnp
from jax import lax
from jax.experimental import pallas as pl
from jax.experimental.pallas import tpu as pltpu
from jax.sharding import PartitionSpec as P

N = 128
D = 72
MESH = pl.DeviceIdType.MESH
HIGH = lax.Precision.HIGHEST


def angles(a, b, g):
    d = b - a
    x = jnp.abs(d)
    y = 2.0 * g
    scale = jnp.where(jnp.maximum(x, jnp.abs(y)) < 2.0**-50, 2.0**80, 1.0)
    x = x * scale
    y = jnp.where(d < 0, -y, y) * scale
    turns = x > 0
    x = jnp.where(turns, x, 1.0)
    y = jnp.where(turns, y, 0.0)
    inv = lax.rsqrt(x * x + y * y)
    c2 = 0.5 + (0.5 * x) * inv
    inv_c = lax.rsqrt(c2)
    return c2 * inv_c, ((0.5 * y) * inv) * inv_c


def fan(x):
    return pltpu.roll(x, 0, 1, stride=1, stride_axis=0)


def fan_back(x):
    row = lax.broadcasted_iota(jnp.int32, x.shape, 0)
    for bit in (1, 2, 4):
        x = jnp.where((row & bit) != 0, pltpu.roll(x, N - bit, 1), x)
    parts = [x[m : m + 8] if m == 0 else pltpu.roll(x[m : m + 8], N - m, 1) for m in range(0, N, 8)]
    return jnp.concatenate(parts, axis=0)


def skew(transposed):
    return fan(fan_back(transposed).T)


def rounds(gram_ref, out_ref, a_ref, b_ref, g_ref, t_ref, ml_ref, mr_ref):
    cross = gram_ref[N : 2 * N]
    a_ref[...] = skew(gram_ref[:N])[:D]
    b_ref[...] = skew(gram_ref[2 * N :])[:D]
    g_ref[pl.ds(N, D), :] = skew(cross.T)[:D]
    t_ref[pl.ds(0, D), :] = skew(cross)[:D]
    ml_ref[...] = jnp.zeros_like(ml_ref)
    mr_ref[...] = jnp.zeros_like(mr_ref)
    ml_ref[0, pl.ds(0, 1), :] = jnp.ones((1, N), jnp.float32)
    mr_ref[1, pl.ds(N, 1), :] = jnp.ones((1, N), jnp.float32)

    def one_round(rows, r, carry):
        c, s = angles(*carry)
        n = max(rows, D)
        cd = fan(jnp.broadcast_to(c, (n, N)))
        sd = fan(jnp.broadcast_to(s, (n, N)))
        a, b = a_ref[...], b_ref[...]
        gw, tw = pl.ds(N - r, D), pl.ds(r, D)
        g, t = g_ref[gw, :], t_ref[tw, :]
        a, t = c * a - s * t, s * a + c * t
        g, b = c * g - s * b, s * g + c * b
        ch, sh = cd[:D], sd[:D]
        a, g = ch * a - sh * g, sh * a + ch * g
        t, b = ch * t - sh * b, sh * t + ch * b
        b = pltpu.roll(b, N - 1, 1)
        t = pltpu.roll(t, N - 1, 1)
        a_ref[...] = a
        b_ref[...] = b
        g_ref[gw, :] = g
        t_ref[tw, :] = t
        g_ref[pl.ds(N - 1 - r, 1), :] = t[1:2]
        t_ref[pl.ds(r + D, 1), :] = pltpu.roll(g[N - D : N - D + 1], D - 1, 1)
        mw = pl.ds(N - r, rows)
        cm, sm = cd[:rows], sd[:rows]
        for h in range(2):
            left, right = ml_ref[h, pl.ds(0, rows), :], mr_ref[h, mw, :]
            ml_ref[h, pl.ds(0, rows), :] = cm * left - sm * right
            mr_ref[h, mw, :] = sm * left + cm * right
        return a[0:1], b[0:1], t[1:2]

    carry = (a_ref[0:1, :], b_ref[0:1, :], t_ref[0:1, :])
    stages = 4
    for stage in range(stages):
        first, last = N * stage // stages, N * (stage + 1) // stages
        carry = lax.fori_loop(first, last, functools.partial(one_round, last), carry)
    for h in range(2):
        mr_ref[h, pl.ds(0, 1), :] = mr_ref[h, pl.ds(N, 1), :]
        out_ref[0:N, h * N : (h + 1) * N] = fan(fan_back(ml_ref[h]).T)
        out_ref[N:, h * N : (h + 1) * N] = fan(fan_back(mr_ref[h, 0:N, :]).T)


ROUND_SCRATCH = [
    pltpu.VMEM((D, N), jnp.float32),
    pltpu.VMEM((D, N), jnp.float32),
    pltpu.VMEM((208, N), jnp.float32),
    pltpu.VMEM((208, N), jnp.float32),
    pltpu.VMEM((2, N, N), jnp.float32),
    pltpu.VMEM((2, 2 * N, N), jnp.float32),
]


def gram_kernel(x_ref, sum_ref, part, half, piece, in_core, in_x, in_z, send, recv_core, recv_x, recv_z, recv_gx, recv_gc):
    me = lax.axis_index("row")
    core, x, z = lax.rem(me, 2), lax.rem(me // 2, 4), me // 8

    def place(z, x, core):
        return {"row": (z * 4 + x) * 2 + core}

    barrier = pltpu.get_barrier_semaphore()
    pl.semaphore_signal(barrier, inc=1, device_id=place(z, x, 1 - core), device_id_type=MESH)
    for k in range(1, 4):
        pl.semaphore_signal(barrier, inc=1, device_id=place(z, lax.rem(x + k, 4), core), device_id_type=MESH)
        pl.semaphore_signal(barrier, inc=1, device_id=place(lax.rem(z + k, 4), x, core), device_id_type=MESH)

    left, right = x_ref[:, :N], x_ref[:, N:]

    def cross(u, v):
        return lax.dot_general(u, v, (((0,), (0,)), ((), ())), precision=HIGH, preferred_element_type=jnp.float32)

    part[:N] = cross(left, left)
    part[N : 2 * N] = cross(left, right)
    part[2 * N :] = cross(right, right)
    pl.semaphore_wait(barrier, 7)

    def copy(src, dst, send_sem, recv_sem, to):
        return pltpu.make_async_remote_copy(
            src_ref=src, dst_ref=dst, send_sem=send_sem, recv_sem=recv_sem, device_id=to, device_id_type=MESH
        )

    h = 3 * N // 2
    q = h // 4
    mine = pl.ds(pl.multiple_of(core * h, 8), h)
    other = pl.ds(pl.multiple_of((1 - core) * h, 8), h)
    sent = []
    c = copy(part.at[other], in_core, send.at[0], recv_core, place(z, x, 1 - core))
    c.start()
    sent.append(c)
    c.wait_recv()
    half[...] = part[mine] + in_core[...]

    quarter = pl.ds(pl.multiple_of(x * q, 8), q)
    for k in range(1, 4):
        xt = lax.rem(x + k, 4)
        c = copy(half.at[pl.ds(pl.multiple_of(xt * q, 8), q)], in_x.at[x], send.at[k], recv_x.at[x], place(z, xt, core))
        c.start()
        sent.append(c)
    in_x[x] = half[quarter]
    for k in range(1, 4):
        xf = lax.rem(x + k, 4)
        copy(in_x.at[xf], in_x.at[xf], send.at[k], recv_x.at[xf], place(z, xf, core)).wait_recv()
    in_z[z] = (in_x[0] + in_x[1]) + (in_x[2] + in_x[3])

    for k in range(1, 4):
        zt = lax.rem(z + k, 4)
        c = copy(in_z.at[z], in_z.at[z], send.at[3 + k], recv_z.at[z], place(zt, x, core))
        c.start()
        sent.append(c)
    for k in range(1, 4):
        zf = lax.rem(z + k, 4)
        copy(in_z.at[zf], in_z.at[zf], send.at[3 + k], recv_z.at[zf], place(zf, x, core)).wait_recv()

    def rows_of(core, x):
        return pl.ds(pl.multiple_of(core * h + x * q, 8), q)

    own = sum_ref.at[rows_of(core, x)]
    own[...] = (in_z[0] + in_z[1]) + (in_z[2] + in_z[3])
    for k in range(1, 4):
        c = copy(own, own, send.at[6 + k], recv_gx.at[x], place(z, lax.rem(x + k, 4), core))
        c.start()
        sent.append(c)
    for k in range(4):
        xf = lax.rem(x + k, 4)
        there = sum_ref.at[rows_of(core, xf)]
        if k:
            copy(there, there, send.at[6 + k], recv_gx.at[xf], place(z, xf, core)).wait_recv()
        c = copy(there, there, send.at[10 + k], recv_gc.at[xf], place(z, x, 1 - core))
        c.start()
        sent.append(c)
    for k in range(4):
        xf = lax.rem(x + k, 4)
        there = sum_ref.at[rows_of(1 - core, xf)]
        copy(there, there, send.at[10 + k], recv_gc.at[xf], place(z, x, 1 - core)).wait_recv()
    for c in sent:
        c.wait_send()


def summed_gram(x):
    q = 3 * N // 8
    dma = pltpu.SemaphoreType.DMA
    return pl.pallas_call(
        gram_kernel,
        out_shape=jax.ShapeDtypeStruct((3 * N, N), jnp.float32),
        in_specs=[pl.BlockSpec(memory_space=pltpu.VMEM)],
        out_specs=pl.BlockSpec(memory_space=pltpu.VMEM),
        scratch_shapes=[
            pltpu.VMEM((3 * N, N), jnp.float32),
            pltpu.VMEM((4 * q, N), jnp.float32),
            pltpu.VMEM((q, N), jnp.float32),
            pltpu.VMEM((4 * q, N), jnp.float32),
            pltpu.VMEM((4, q, N), jnp.float32),
            pltpu.VMEM((4, q, N), jnp.float32),
            dma((14,)),
            dma,
            dma((4,)),
            dma((4,)),
            dma((4,)),
            dma((4,)),
        ],
        compiler_params=pltpu.CompilerParams(collective_id=0, has_side_effects=True, vmem_limit_bytes=40 << 20),
        name="gram_sum",
    )(x)


def jacobi_rounds(gram):
    return pl.pallas_call(
        rounds,
        out_shape=jax.ShapeDtypeStruct((2 * N, 2 * N), jnp.float32),
        in_specs=[pl.BlockSpec(memory_space=pltpu.VMEM)],
        out_specs=pl.BlockSpec(memory_space=pltpu.VMEM),
        scratch_shapes=ROUND_SCRATCH,
        compiler_params=pltpu.CompilerParams(vmem_limit_bytes=40 << 20),
        name="jacobi_rounds",
    )(gram)


CHUNKS = 8


def move_kernel(x_ref, m_ref, out_ref, y, send_f, send_b, recv_f, recv_b, local):
    k = lax.axis_index("pair")
    last = lax.axis_size("pair") - 1
    barrier = pltpu.get_barrier_semaphore()
    after, before = lax.rem(k + 1, last + 1), lax.rem(k + last, last + 1)
    for to in (after, before):
        pl.semaphore_signal(barrier, inc=1, device_id={"pair": to}, device_id_type=MESH)
    pl.semaphore_wait(barrier, 2)
    rows = x_ref.shape[0] // CHUNKS

    def forward(j):
        at = pl.ds(j * rows, rows)
        return pltpu.make_async_remote_copy(
            src_ref=y.at[jnp.where(k == 0, 1, 0), at], dst_ref=out_ref.at[at, pl.ds(0, N)],
            send_sem=send_f.at[j], recv_sem=recv_f.at[j], device_id={"pair": after}, device_id_type=MESH,
        )

    def backward(j):
        at = pl.ds(j * rows, rows)
        return pltpu.make_async_remote_copy(
            src_ref=y.at[1, at], dst_ref=out_ref.at[at, pl.ds(N, N)],
            send_sem=send_b.at[j], recv_sem=recv_b.at[j], device_id={"pair": before}, device_id_type=MESH,
        )

    keep_left = pltpu.make_async_copy(y.at[0], out_ref.at[:, pl.ds(0, N)], local)
    keep_right = pltpu.make_async_copy(y.at[0], out_ref.at[:, pl.ds(N, N)], local)

    for j in range(CHUNKS):
        at = pl.ds(j * rows, rows)
        moved = lax.dot_general(
            x_ref[at, :], m_ref[...], (((1,), (1,)), ((), ())), precision=HIGH, preferred_element_type=jnp.float32
        )
        y[0, at] = moved[:, :N]
        y[1, at] = moved[:, N:]
        pl.when(k < last)(lambda: forward(j).start())
        pl.when(k > 0)(lambda: backward(j).start())
    pl.when(k == 0)(lambda: keep_left.start())
    pl.when(k == last)(lambda: keep_right.start())
    for j in range(CHUNKS):
        pl.when(k < last)(lambda: forward(j).wait_send())
        pl.when(k > 0)(lambda: backward(j).wait_send())
        pl.when(k > 0)(lambda: forward(j).wait_recv())
        pl.when(k < last)(lambda: backward(j).wait_recv())
    pl.when(k == 0)(lambda: keep_left.wait())
    pl.when(k == last)(lambda: keep_right.wait())


def mixed_and_moved(x, mixing):
    dma = pltpu.SemaphoreType.DMA
    return pl.pallas_call(
        move_kernel,
        out_shape=jax.ShapeDtypeStruct(x.shape, jnp.float32),
        in_specs=[pl.BlockSpec(memory_space=pltpu.VMEM)] * 2,
        out_specs=pl.BlockSpec(memory_space=pl.ANY),
        scratch_shapes=[pltpu.VMEM((2, x.shape[0], N), jnp.float32)] + [dma((CHUNKS,))] * 4 + [dma],
        compiler_params=pltpu.CompilerParams(collective_id=1, has_side_effects=True, vmem_limit_bytes=40 << 20),
        name="mix_and_move",
    )(x, mixing)


def per_device(matrix):
    return mixed_and_moved(matrix, jacobi_rounds(summed_gram(matrix)))


def solution(mesh):
    return jax.shard_map(
        per_device, mesh=mesh, in_specs=(P("row", "pair"),), out_specs=P("row", "pair"), check_vma=False
    )
```

time: 552 us -> 113 us (0.20)
  the two profiles are of different devices: /device:TPU:1 before, /device:TPU:112 now
where the time goes in v1:
time: 113 us
  Pallas kernels  110 us (97%)
  local copies, waits for them, and re-layouts  2.92 us (3%)
    pallas_call x1, Pallas kernels, mixed_and_moved(): pl.pallas_call(move_kernel, out_shape=jax.ShapeDtypeStruct(x.shape, jnp.f...  52.5 us
    pallas_call x1, Pallas kernels, summed_gram(): pl.pallas_call(gram_kernel, out_shape=jax.ShapeDtypeStruct((3 * N, N), jn...  29.4 us
    pallas_call x1, Pallas kernels, jacobi_rounds(): pl.pallas_call(rounds, out_shape=jax.ShapeDtypeStruct((2 * N, 2 * N), jnp...  28.1 us
    unnamed x5, local copies, waits for them, and re-layouts  2.92 us

profile of v1, /device:TPU:112, one launch (start us, length us, event | category | flops | bytes accessed | tf_op | source)
XLA Modules:
  0.0 113.0 jit_solution(3375545628175188342)
XLA Ops:
  0.0 0.0 copy-start
  0.0 1.6 %copy-done = f32[2048,256]{1,0:T(8,128)S(1)} copy-done((f32[2048,256]{1,0:T(8,128)S(1)}, f32[2048,256]{1,0:T(8,128)}, u32[]{:S(2)}) %copy-start) | copy-done | bytes 2097176
  1.6 0.0 copy-start.1
  1.6 29.4 %gram_sum.1.gram_ref = f32[384,128]{1,0:T(8,128)S(1)} custom-call(f32[2048,256]{1,0:T(8,128)S(1)} %copy-done), custom_call_target="tpu_custom_call" | custom-call | tf_op jit(solution)/shard_map/gram_sum/pallas_call | solution.py:197
  31.1 28.1 %jacobi_rounds.1.m_ref = f32[256,256]{1,0:T(8,128)S(1)} custom-call(f32[384,128]{1,0:T(8,128)S(1)} %gram_sum.1.gram_ref), custom_call_target="tpu_custom_call" | custom-call | tf_op jit(solution)/shard_map/jacobi_rounds/pallas_call | solution.py:222
  59.2 0.0 copy-done.1
  59.2 52.5 %mix_and_move.1 = f32[2048,256]{1,0:T(8,128)S(1)} custom-call(f32[2048,256]{1,0:T(8,128)S(1)} %copy-done.1, f32[256,256]{1,0:T(8,128)S(1)} %jacobi_rounds.1.m_ref), custom_call_target="tpu_custom_call" | custom-call | tf_op jit(solution)/shard_map/mix_and_move/pallas_call | solution.py:285
  111.7 1.3 %copy.3 = f32[2048,256]{1,0:T(8,128)} copy(f32[2048,256]{1,0:T(8,128)S(1)} %mix_and_move.1) | data formatting | bytes 4194304
Async XLA Ops:
  0.0 1.6 %copy-start = (f32[2048,256]{1,0:T(8,128)S(1)}, f32[2048,256]{1,0:T(8,128)}, u32[]{:S(2)}) copy-start(f32[2048,256]{1,0:T(8,128)} %x_ref.3) | copy-start | bytes 6291460
  1.6 57.6 %copy-start.1 = (f32[2048,256]{1,0:T(8,128)S(1)}, f32[2048,256]{1,0:T(8,128)}, u32[]{:S(2)}) copy-start(f32[2048,256]{1,0:T(8,128)} %x_ref.3) | copy-start | bytes 6291460

commit v2 on v1

v2 whole, which is shorter than its diff:
```python
import functools

import jax
import jax.numpy as jnp
from jax import lax
from jax.experimental import pallas as pl
from jax.experimental.pallas import tpu as pltpu
from jax.sharding import PartitionSpec as P

N = 128
D = 72
MESH = pl.DeviceIdType.MESH
HIGH = lax.Precision.HIGHEST


def angles(a, b, g):
    d = b - a
    x = jnp.abs(d)
    y = 2.0 * g
    scale = jnp.where(jnp.maximum(x, jnp.abs(y)) < 2.0**-50, 2.0**80, 1.0)
    x = x * scale
    y = jnp.where(d < 0, -y, y) * scale
    turns = x > 0
    x = jnp.where(turns, x, 1.0)
    y = jnp.where(turns, y, 0.0)
    inv = lax.rsqrt(x * x + y * y)
    c2 = 0.5 + (0.5 * x) * inv
    inv_c = lax.rsqrt(c2)
    return c2 * inv_c, ((0.5 * y) * inv) * inv_c


def fan(x):
    return pltpu.roll(x, 0, 1, stride=1, stride_axis=0)


def fan_back(x):
    row = lax.broadcasted_iota(jnp.int32, x.shape, 0)
    for bit in (1, 2, 4):
        x = jnp.where((row & bit) != 0, pltpu.roll(x, N - bit, 1), x)
    parts = [x[m : m + 8] if m == 0 else pltpu.roll(x[m : m + 8], N - m, 1) for m in range(0, N, 8)]
    return jnp.concatenate(parts, axis=0)


def skew(transposed):
    return fan(fan_back(transposed).T)


def rounds(gram_ref, out_ref, a_ref, b_ref, g_ref, t_ref, ml_ref, mr_ref):
    cross = gram_ref[N : 2 * N]
    a_ref[...] = skew(gram_ref[:N])[:D]
    b_ref[...] = skew(gram_ref[2 * N :])[:D]
    g_ref[pl.ds(N, D), :] = skew(cross.T)[:D]
    t_ref[pl.ds(0, D), :] = skew(cross)[:D]
    ml_ref[...] = jnp.zeros_like(ml_ref)
    mr_ref[...] = jnp.zeros_like(mr_ref)
    ml_ref[0, pl.ds(0, 1), :] = jnp.ones((1, N), jnp.float32)
    mr_ref[1, pl.ds(N, 1), :] = jnp.ones((1, N), jnp.float32)

    def one_round(rows, r, carry):
        c, s = angles(*carry)
        n = max(rows, D)
        cd = fan(jnp.broadcast_to(c, (n, N)))
        sd = fan(jnp.broadcast_to(s, (n, N)))
        a, b = a_ref[...], b_ref[...]
        gw, tw = pl.ds(N - r, D), pl.ds(r, D)
        g, t = g_ref[gw, :], t_ref[tw, :]
        a, t = c * a - s * t, s * a + c * t
        g, b = c * g - s * b, s * g + c * b
        ch, sh = cd[:D], sd[:D]
        a, g = ch * a - sh * g, sh * a + ch * g
        t, b = ch * t - sh * b, sh * t + ch * b
        b = pltpu.roll(b, N - 1, 1)
        t = pltpu.roll(t, N - 1, 1)
        a_ref[...] = a
        b_ref[...] = b
        g_ref[gw, :] = g
        t_ref[tw, :] = t
        g_ref[pl.ds(N - 1 - r, 1), :] = t[1:2]
        t_ref[pl.ds(r + D, 1), :] = pltpu.roll(g[N - D : N - D + 1], D - 1, 1)
        mw = pl.ds(N - r, rows)
        cm, sm = cd[:rows], sd[:rows]
        for h in range(2):
            left, right = ml_ref[h, pl.ds(0, rows), :], mr_ref[h, mw, :]
            ml_ref[h, pl.ds(0, rows), :] = cm * left - sm * right
            mr_ref[h, mw, :] = sm * left + cm * right
        return a[0:1], b[0:1], t[1:2]

    carry = (a_ref[0:1, :], b_ref[0:1, :], t_ref[0:1, :])
    stages = 4
    for stage in range(stages):
        first, last = N * stage // stages, N * (stage + 1) // stages
        carry = lax.fori_loop(first, last, functools.partial(one_round, last), carry)
    for h in range(2):
        mr_ref[h, pl.ds(0, 1), :] = mr_ref[h, pl.ds(N, 1), :]
        out_ref[0:N, h * N : (h + 1) * N] = fan(fan_back(ml_ref[h]).T)
        out_ref[N:, h * N : (h + 1) * N] = fan(fan_back(mr_ref[h, 0:N, :]).T)


ROUND_SCRATCH = [
    pltpu.VMEM((D, N), jnp.float32),
    pltpu.VMEM((D, N), jnp.float32),
    pltpu.VMEM((208, N), jnp.float32),
    pltpu.VMEM((208, N), jnp.float32),
    pltpu.VMEM((2, N, N), jnp.float32),
    pltpu.VMEM((2, 2 * N, N), jnp.float32),
]


EARLY = 640
RAW_PARTS = 2
RAW_AT = 0
LATE = (128, 128, 256, 256, 256, 384)
STARTS = tuple(EARLY + sum(LATE[:i]) for i in range(len(LATE)))
LOADS = 4


def remote(src, dst, send_sem, recv_sem, to):
    return pltpu.make_async_remote_copy(
        src_ref=src, dst_ref=dst, send_sem=send_sem, recv_sem=recv_sem, device_id=to, device_id_type=MESH
    )


def mixed(rows, mixing):
    return lax.dot_general(
        rows, mixing, (((1,), (1,)), ((), ())), precision=HIGH, preferred_element_type=jnp.float32
    )


def partial_gram(x_ref, xb, part, load):
    size = xb.shape[0] // LOADS
    copies = []
    for j in range(LOADS):
        at = pl.ds(j * size, size)
        copies.append(pltpu.make_async_copy(x_ref.at[at], xb.at[at], load.at[j]))
        copies[-1].start()

    def cross(u, v):
        return lax.dot_general(u, v, (((0,), (0,)), ((), ())), preferred_element_type=jnp.float32)

    even = odd = 0.0
    for j in range(LOADS):
        copies[j].wait()
        x = xb[pl.ds(j * size, size), :]
        high = x.astype(jnp.bfloat16)
        rest = x - high.astype(jnp.float32)
        mid = rest.astype(jnp.bfloat16)
        low = (rest - mid.astype(jnp.float32)).astype(jnp.bfloat16)
        even = even + (cross(high, high) + cross(mid, mid))
        odd = odd + (cross(high, mid) + cross(high, low))
    gram = even + (odd + odd.T)
    part[:N] = gram[:N, :N]
    part[N : 2 * N] = gram[:N, N:]
    part[2 * N :] = gram[N:, N:]


def step_kernel(x_ref, out_ref, xb, y, raw, raw_y, part, half, total, in_core, in_x, in_z, mix, near, round_refs, sems):
    me, k = lax.axis_index("row"), lax.axis_index("pair")
    core, x, z = lax.rem(me, 2), lax.rem(me // 2, 4), me // 8
    last = lax.axis_size("pair") - 1
    after, before = lax.rem(k + 1, last + 1), lax.rem(k + last, last + 1)
    load, send, recv_core, recv_x, recv_z, recv_gx, recv_gc, raw_send, raw_recv, mix_send, mix_recv, late_send, late_recv, keep = sems

    def place(z, x, core):
        return {"row": (z * 4 + x) * 2 + core}

    def peer(i):
        other = lax.rem(me + i, 8)
        return other, {"row": z * 8 + other}

    barrier = pltpu.get_barrier_semaphore()
    for i in range(1, 8):
        pl.semaphore_signal(barrier, inc=1, device_id=peer(i)[1], device_id_type=MESH)
    for i in range(1, 4):
        pl.semaphore_signal(barrier, inc=1, device_id=place(lax.rem(z + i, 4), x, core), device_id_type=MESH)
    for to in (after, before):
        pl.semaphore_signal(barrier, inc=1, device_id={"pair": to}, device_id_type=MESH)

    partial_gram(x_ref, xb, part, load)
    pl.semaphore_wait(barrier, 12)

    h = 3 * N // 2
    q = h // 4
    mine = pl.ds(pl.multiple_of(core * h, 8), h)
    other = pl.ds(pl.multiple_of((1 - core) * h, 8), h)
    sent = []
    c = remote(part.at[other], in_core, send.at[0], recv_core, place(z, x, 1 - core))
    c.start()
    sent.append(c)

    size = EARLY // RAW_PARTS
    raw_f, raw_b = [], []
    for j in range(RAW_PARTS):
        at = pl.ds(j * size, size)
        raw_f.append(remote(xb.at[at], raw.at[0, at], raw_send.at[0, j], raw_recv.at[0, j], {"pair": after}))
        raw_b.append(remote(xb.at[at], raw.at[1, at], raw_send.at[1, j], raw_recv.at[1, j], {"pair": before}))

    def start_raw():
        for j in range(RAW_PARTS):
            pl.when(k < last)(raw_f[j].start)
            pl.when(k > 0)(raw_b[j].start)

    if RAW_AT == 0:
        start_raw()
    c.wait_recv()
    half[...] = part[mine] + in_core[...]

    quarter = pl.ds(pl.multiple_of(x * q, 8), q)
    for i in range(1, 4):
        xt = lax.rem(x + i, 4)
        c = remote(half.at[pl.ds(pl.multiple_of(xt * q, 8), q)], in_x.at[x], send.at[i], recv_x.at[x], place(z, xt, core))
        c.start()
        sent.append(c)
    in_x[x] = half[quarter]
    for i in range(1, 4):
        xf = lax.rem(x + i, 4)
        remote(in_x.at[xf], in_x.at[xf], send.at[i], recv_x.at[xf], place(z, xf, core)).wait_recv()
    in_z[z] = (in_x[0] + in_x[1]) + (in_x[2] + in_x[3])

    for i in range(1, 4):
        zt = lax.rem(z + i, 4)
        c = remote(in_z.at[z], in_z.at[z], send.at[3 + i], recv_z.at[z], place(zt, x, core))
        c.start()
        sent.append(c)
    if RAW_AT == 1:
        start_raw()
    for i in range(1, 4):
        zf = lax.rem(z + i, 4)
        remote(in_z.at[zf], in_z.at[zf], send.at[3 + i], recv_z.at[zf], place(zf, x, core)).wait_recv()
    if RAW_AT == 2:
        start_raw()

    def rows_of(core, x):
        return total.at[pl.ds(pl.multiple_of(core * h + x * q, 8), q)]

    own = rows_of(core, x)
    own[...] = (in_z[0] + in_z[1]) + (in_z[2] + in_z[3])
    for i in range(1, 4):
        c = remote(own, own, send.at[6 + i], recv_gx.at[x], place(z, lax.rem(x + i, 4), core))
        c.start()
        sent.append(c)
    for i in range(4):
        xf = lax.rem(x + i, 4)
        there = rows_of(core, xf)
        if i:
            remote(there, there, send.at[6 + i], recv_gx.at[xf], place(z, xf, core)).wait_recv()
        c = remote(there, there, send.at[10 + i], recv_gc.at[xf], place(z, x, 1 - core))
        c.start()
        sent.append(c)
    for i in range(4):
        xf = lax.rem(x + i, 4)
        there = rows_of(1 - core, xf)
        remote(there, there, send.at[10 + i], recv_gc.at[xf], place(z, x, 1 - core)).wait_recv()
    for c in sent:
        c.wait_send()

    rounds(total, mix, *round_refs)

    seat = lax.rem(me, 8)
    share = N // 8

    def eighth(i):
        return pl.ds(pl.multiple_of(i * share, 8), share)

    first = jnp.where(k == 0, N, 0)
    mix_f = remote(
        mix.at[pl.ds(pl.multiple_of(first + seat * share, 8), share)], near.at[0, eighth(seat)],
        mix_send.at[0, 0], mix_recv.at[0, seat], {"pair": after},
    )
    mix_b = remote(
        mix.at[pl.ds(pl.multiple_of(N + seat * share, 8), share)], near.at[1, eighth(seat)],
        mix_send.at[1, 0], mix_recv.at[1, seat], {"pair": before},
    )
    pl.when(k < last)(mix_f.start)
    pl.when(k > 0)(mix_b.start)

    late_f, late_b = [], []
    for j, (start, size) in enumerate(zip(STARTS, LATE)):
        at = pl.ds(start, size)
        late_f.append(remote(y.at[jnp.where(k == 0, 1, 0), at], out_ref.at[at, pl.ds(0, N)], late_send.at[0, j], late_recv.at[0, j], {"pair": after}))
        late_b.append(remote(y.at[1, at], out_ref.at[at, pl.ds(N, N)], late_send.at[1, j], late_recv.at[1, j], {"pair": before}))

    def spread(which):
        for i in range(1, 8):
            to = peer(i)[1]
            remote(near.at[which, eighth(seat)], near.at[which, eighth(seat)], mix_send.at[which, i], mix_recv.at[which, seat], to).start()

    def rotate(at):
        moved = mixed(xb[at, :], mix[...])
        y[0, at] = moved[:, :N]
        y[1, at] = moved[:, N:]

    for j, (start, size) in enumerate(zip(STARTS, LATE)):
        rotate(pl.ds(start, size))
        pl.when(k < last)(late_f[j].start)
        pl.when(k > 0)(late_b[j].start)

    @pl.when(k > 0)
    def _():
        mix_f.wait_recv()
        spread(0)

    @pl.when(k < last)
    def _():
        mix_b.wait_recv()
        spread(1)

    keep_left = pltpu.make_async_copy(y.at[0], out_ref.at[:, pl.ds(0, N)], keep.at[0])
    keep_right = pltpu.make_async_copy(y.at[0], out_ref.at[:, pl.ds(N, N)], keep.at[1])

    @pl.when((k == 0) | (k == last))
    def _():
        rotate(pl.ds(0, EARLY))

    pl.when(k == 0)(keep_left.start)
    pl.when(k == last)(keep_right.start)

    def finish(which, copies):
        for c in copies:
            c.wait_recv()
        for i in range(1, 8):
            there, device = peer(i)
            slot = near.at[which, eighth(there)]
            remote(slot, slot, mix_send.at[which, i], mix_recv.at[which, there], device).wait_recv()
        raw_y[which] = mixed(raw[which], near[which])
        c = pltpu.make_async_copy(raw_y.at[which], out_ref.at[pl.ds(0, EARLY), pl.ds(which * N, N)], keep.at[which])
        c.start()
        for i in range(1, 8):
            slot = near.at[which, eighth(seat)]
            remote(slot, slot, mix_send.at[which, i], mix_recv.at[which, seat], peer(i)[1]).wait_send()

    pl.when(k > 0)(lambda: finish(0, raw_f))
    pl.when(k < last)(lambda: finish(1, raw_b))

    for c in [mix_f] + raw_f + late_f:
        pl.when(k < last)(c.wait_send)
    for c in [mix_b] + raw_b + late_b:
        pl.when(k > 0)(c.wait_send)
    for c in late_f:
        pl.when(k > 0)(c.wait_recv)
    for c in late_b:
        pl.when(k < last)(c.wait_recv)
    early_left = pltpu.make_async_copy(raw_y.at[0], out_ref.at[pl.ds(0, EARLY), pl.ds(0, N)], keep.at[0])
    early_right = pltpu.make_async_copy(raw_y.at[1], out_ref.at[pl.ds(0, EARLY), pl.ds(N, N)], keep.at[1])
    pl.when(k == 0)(keep_left.wait)
    pl.when(k > 0)(early_left.wait)
    pl.when(k == last)(keep_right.wait)
    pl.when(k < last)(early_right.wait)


def per_device(matrix):
    rows = matrix.shape[0]
    q = 3 * N // 8
    dma = pltpu.SemaphoreType.DMA
    f32 = jnp.float32
    return pl.pallas_call(
        step_kernel,
        out_shape=jax.ShapeDtypeStruct(matrix.shape, f32),
        in_specs=[pl.BlockSpec(memory_space=pl.ANY)],
        out_specs=pl.BlockSpec(memory_space=pl.ANY),
        scratch_shapes=[
            pltpu.VMEM((rows, 2 * N), f32),
            pltpu.VMEM((2, rows, N), f32),
            pltpu.VMEM((2, EARLY, 2 * N), f32),
            pltpu.VMEM((2, EARLY, N), f32),
            pltpu.VMEM((3 * N, N), f32),
            pltpu.VMEM((4 * q, N), f32),
            pltpu.VMEM((3 * N, N), f32),
            pltpu.VMEM((4 * q, N), f32),
            pltpu.VMEM((4, q, N), f32),
            pltpu.VMEM((4, q, N), f32),
            pltpu.VMEM((2 * N, 2 * N), f32),
            pltpu.VMEM((2, N, 2 * N), f32),
            ROUND_SCRATCH,
            [
                dma((LOADS,)),
                dma((14,)),
                dma,
                dma((4,)),
                dma((4,)),
                dma((4,)),
                dma((4,)),
                dma((2, RAW_PARTS)),
                dma((2, RAW_PARTS)),
                dma((2, 8)),
                dma((2, 8)),
                dma((2, len(LATE))),
                dma((2, len(LATE))),
                dma((2,)),
            ],
        ],
        compiler_params=pltpu.CompilerParams(collective_id=0, has_side_effects=True, vmem_limit_bytes=48 << 20),
        name="jacobi_step",
    )(matrix)


def solution(mesh):
    return jax.shard_map(
        per_device, mesh=mesh, in_specs=(P("row", "pair"),), out_specs=P("row", "pair"), check_vma=False
    )
```

time: 113 us -> 121 us (1.071)
  the two profiles are of different devices: /device:TPU:112 before, /device:TPU:1 now
where the time goes in v2:
time: 121 us
  Pallas kernels  118 us (98%)
  local copies, waits for them, and re-layouts  2.91 us (2%)
    pallas_call x1, Pallas kernels, per_device(): pl.pallas_call(step_kernel, out_shape=jax.ShapeDtypeStruct(matrix.shape,...  118 us
    unnamed x3, local copies, waits for them, and re-layouts  2.91 us

profile of v2, /device:TPU:1, one launch (start us, length us, event | category | flops | bytes accessed | tf_op | source)
XLA Modules:
  0.0 120.8 jit_solution(14522531688969693567)
XLA Ops:
  0.0 0.0 copy-start
  0.0 1.6 %copy-done = f32[2048,256]{1,0:T(8,128)S(1)} copy-done((f32[2048,256]{1,0:T(8,128)S(1)}, f32[2048,256]{1,0:T(8,128)}, u32[]{:S(2)}) %copy-start) | copy-done | bytes 2097176
  1.6 117.9 %jacobi_step.1 = f32[2048,256]{1,0:T(8,128)S(1)} custom-call(f32[2048,256]{1,0:T(8,128)S(1)} %copy-done), custom_call_target="tpu_custom_call" | custom-call | tf_op jit(solution)/shard_map/jacobi_step/pallas_call | solution.py:355
  119.5 1.3 %copy.3 = f32[2048,256]{1,0:T(8,128)} copy(f32[2048,256]{1,0:T(8,128)S(1)} %jacobi_step.1) | data formatting | bytes 4194304
Async XLA Ops:
  0.0 1.6 %copy-start = (f32[2048,256]{1,0:T(8,128)S(1)}, f32[2048,256]{1,0:T(8,128)}, u32[]{:S(2)}) copy-start(f32[2048,256]{1,0:T(8,128)} %x_ref.1) | copy-start | bytes 6291460

commit v3 on v2

--- a/solution.py
+++ b/solution.py
@@ -9,6 +9,8 @@
 
 N = 128
 D = 72
+STAGES = 8
+UNROLL = 8
 MESH = pl.DeviceIdType.MESH
 HIGH = lax.Precision.HIGHEST
 
@@ -56,8 +58,16 @@
     ml_ref[0, pl.ds(0, 1), :] = jnp.ones((1, N), jnp.float32)
     mr_ref[1, pl.ds(N, 1), :] = jnp.ones((1, N), jnp.float32)
 
+    def back(x, lanes):
+        return pltpu.roll(x, N - lanes, 1)
+
     def one_round(rows, r, carry):
-        c, s = angles(*carry)
+        da, db, dg, ea, eb, eg, a1, t1, g1, b1 = carry
+        c, s = angles(da, db, dg)
+        ce, se = back(c, 1), back(s, 1)
+        na = c * (c * da - s * dg) - s * (c * dg - s * db)
+        nb = se * (se * ea + ce * eg) + ce * (se * eg + ce * eb)
+        ng = c * (se * a1 + ce * t1) - s * (se * g1 + ce * b1)
         n = max(rows, D)
         cd = fan(jnp.broadcast_to(c, (n, N)))
         sd = fan(jnp.broadcast_to(s, (n, N)))
@@ -69,27 +79,33 @@
         ch, sh = cd[:D], sd[:D]
         a, g = ch * a - sh * g, sh * a + ch * g
         t, b = ch * t - sh * b, sh * t + ch * b
-        b = pltpu.roll(b, N - 1, 1)
-        t = pltpu.roll(t, N - 1, 1)
+        ahead = (back(na, 1), back(nb, 1), back(ng, 1), back(a[1:2], 1), back(t[2:3], 2), back(g[0:1], 1), back(b[1:2], 2))
+        b = back(b, 1)
+        t = back(t, 1)
         a_ref[...] = a
         b_ref[...] = b
         g_ref[gw, :] = g
         t_ref[tw, :] = t
         g_ref[pl.ds(N - 1 - r, 1), :] = t[1:2]
-        t_ref[pl.ds(r + D, 1), :] = pltpu.roll(g[N - D : N - D + 1], D - 1, 1)
+        t_ref[pl.ds(r + D, 1), :] = back(g[N - D : N - D + 1], N - D + 1)
         mw = pl.ds(N - r, rows)
         cm, sm = cd[:rows], sd[:rows]
         for h in range(2):
             left, right = ml_ref[h, pl.ds(0, rows), :], mr_ref[h, mw, :]
             ml_ref[h, pl.ds(0, rows), :] = cm * left - sm * right
             mr_ref[h, mw, :] = sm * left + cm * right
-        return a[0:1], b[0:1], t[1:2]
-
-    carry = (a_ref[0:1, :], b_ref[0:1, :], t_ref[0:1, :])
-    stages = 4
-    for stage in range(stages):
-        first, last = N * stage // stages, N * (stage + 1) // stages
-        carry = lax.fori_loop(first, last, functools.partial(one_round, last), carry)
+        return (na, nb, ng) + ahead
+
+    def group(rows, i, carry):
+        for u in range(UNROLL):
+            carry = one_round(rows, UNROLL * i + u, carry)
+        return carry
+
+    first = (a_ref[0:1, :], b_ref[0:1, :], t_ref[0:1, :])
+    carry = first + tuple(back(v, 1) for v in first + (a_ref[1:2, :], t_ref[1:2, :], g_ref[N + 1 : N + 2, :], b_ref[1:2, :]))
+    for stage in range(STAGES):
+        begin, end = N * stage // STAGES, N * (stage + 1) // STAGES
+        carry = lax.fori_loop(begin // UNROLL, end // UNROLL, functools.partial(group, end), carry)
     for h in range(2):
         mr_ref[h, pl.ds(0, 1), :] = mr_ref[h, pl.ds(N, 1), :]
         out_ref[0:N, h * N : (h + 1) * N] = fan(fan_back(ml_ref[h]).T)
@@ -106,11 +122,13 @@
 ]
 
 
-EARLY = 640
-RAW_PARTS = 2
-RAW_AT = 0
-LATE = (128, 128, 256, 256, 256, 384)
-STARTS = tuple(EARLY + sum(LATE[:i]) for i in range(len(LATE)))
+EARLY = 1024
+RAW_PARTS = 4
+RAW_AT = 2
+CHUNK = 256
+CHUNKS = 8
+QUARTER = CHUNK // 4
+ORDER = tuple(range(EARLY // CHUNK, CHUNKS)) + tuple(range(EARLY // CHUNK))
 LOADS = 4
 
 
@@ -153,12 +171,27 @@
     part[2 * N :] = gram[N:, N:]
 
 
-def step_kernel(x_ref, out_ref, xb, y, raw, raw_y, part, half, total, in_core, in_x, in_z, mix, near, round_refs, sems):
+def step_kernel(x_ref, out_ref, xb, y, raw, raw_y, relay, part, half, total, in_core, in_x, in_z, mix, near, round_refs, sems):
     me, k = lax.axis_index("row"), lax.axis_index("pair")
     core, x, z = lax.rem(me, 2), lax.rem(me // 2, 4), me // 8
     last = lax.axis_size("pair") - 1
-    after, before = lax.rem(k + 1, last + 1), lax.rem(k + last, last + 1)
-    load, send, recv_core, recv_x, recv_z, recv_gx, recv_gc, raw_send, raw_recv, mix_send, mix_recv, late_send, late_recv, keep = sems
+    py, pz = k // 4, lax.rem(k, 4)
+    to_after, to_before = pz < 3, pz > 0
+
+    def pair(distance):
+        return {"pair": lax.rem(k + distance + last + 1, last + 1)}
+
+    after, before = pair(1), pair(-1)
+    top = pz == 3
+    edge = top | (pz == 0)
+    wraps = (top & (py < 3)) | ((pz == 0) & (py > 0))
+    step = jnp.where(top, 1, -1)
+    direct_mine = jnp.where(top, 3 - py, py)
+    direct_passed = jnp.where(top, 4 - py, py + 1)
+    column_mine = pl.ds(pl.multiple_of(jnp.where(top, 0, N), N), N)
+    column_here = pl.ds(pl.multiple_of(jnp.where(top, N, 0), N), N)
+    half_mine = jnp.where(top, 0, 1)
+    load, send, recv_core, recv_x, recv_z, recv_gx, recv_gc, raw_send, raw_recv, mix_send, mix_recv, late_send, late_recv, wrap_send, wrap_recv, relay_send, relay_recv, keep = sems
 
     def place(z, x, core):
         return {"row": (z * 4 + x) * 2 + core}
@@ -172,11 +205,11 @@
         pl.semaphore_signal(barrier, inc=1, device_id=peer(i)[1], device_id_type=MESH)
     for i in range(1, 4):
         pl.semaphore_signal(barrier, inc=1, device_id=place(lax.rem(z + i, 4), x, core), device_id_type=MESH)
-    for to in (after, before):
-        pl.semaphore_signal(barrier, inc=1, device_id={"pair": to}, device_id_type=MESH)
+    for distance in (1, -1, 3, -3, 4, -4):
+        pl.semaphore_signal(barrier, inc=1, device_id=pair(distance), device_id_type=MESH)
 
     partial_gram(x_ref, xb, part, load)
-    pl.semaphore_wait(barrier, 12)
+    pl.semaphore_wait(barrier, 16)
 
     h = 3 * N // 2
     q = h // 4
@@ -191,13 +224,13 @@
     raw_f, raw_b = [], []
     for j in range(RAW_PARTS):
         at = pl.ds(j * size, size)
-        raw_f.append(remote(xb.at[at], raw.at[0, at], raw_send.at[0, j], raw_recv.at[0, j], {"pair": after}))
-        raw_b.append(remote(xb.at[at], raw.at[1, at], raw_send.at[1, j], raw_recv.at[1, j], {"pair": before}))
+        raw_f.append(remote(xb.at[at], raw.at[0, at], raw_send.at[0, j], raw_recv.at[0, j], after))
+        raw_b.append(remote(xb.at[at], raw.at[1, at], raw_send.at[1, j], raw_recv.at[1, j], before))
 
     def start_raw():
         for j in range(RAW_PARTS):
-            pl.when(k < last)(raw_f[j].start)
-            pl.when(k > 0)(raw_b[j].start)
+            pl.when(to_after)(raw_f[j].start)
+            pl.when(to_before)(raw_b[j].start)
 
     if RAW_AT == 0:
         start_raw()
@@ -264,55 +297,92 @@
     first = jnp.where(k == 0, N, 0)
     mix_f = remote(
         mix.at[pl.ds(pl.multiple_of(first + seat * share, 8), share)], near.at[0, eighth(seat)],
-        mix_send.at[0, 0], mix_recv.at[0, seat], {"pair": after},
+        mix_send.at[0, 0], mix_recv.at[0, seat], after,
     )
     mix_b = remote(
         mix.at[pl.ds(pl.multiple_of(N + seat * share, 8), share)], near.at[1, eighth(seat)],
-        mix_send.at[1, 0], mix_recv.at[1, seat], {"pair": before},
+        mix_send.at[1, 0], mix_recv.at[1, seat], before,
     )
-    pl.when(k < last)(mix_f.start)
-    pl.when(k > 0)(mix_b.start)
-
-    late_f, late_b = [], []
-    for j, (start, size) in enumerate(zip(STARTS, LATE)):
-        at = pl.ds(start, size)
-        late_f.append(remote(y.at[jnp.where(k == 0, 1, 0), at], out_ref.at[at, pl.ds(0, N)], late_send.at[0, j], late_recv.at[0, j], {"pair": after}))
-        late_b.append(remote(y.at[1, at], out_ref.at[at, pl.ds(N, N)], late_send.at[1, j], late_recv.at[1, j], {"pair": before}))
-
-    def spread(which):
-        for i in range(1, 8):
-            to = peer(i)[1]
-            remote(near.at[which, eighth(seat)], near.at[which, eighth(seat)], mix_send.at[which, i], mix_recv.at[which, seat], to).start()
-
-    def rotate(at):
-        moved = mixed(xb[at, :], mix[...])
-        y[0, at] = moved[:, :N]
-        y[1, at] = moved[:, N:]
-
-    for j, (start, size) in enumerate(zip(STARTS, LATE)):
-        rotate(pl.ds(start, size))
-        pl.when(k < last)(late_f[j].start)
-        pl.when(k > 0)(late_b[j].start)
-
-    @pl.when(k > 0)
-    def _():
-        mix_f.wait_recv()
-        spread(0)
-
-    @pl.when(k < last)
-    def _():
-        mix_b.wait_recv()
-        spread(1)
+    pl.when(to_after)(mix_f.start)
+    pl.when(to_before)(mix_b.start)
+
+    def chunk(c):
+        return pl.ds(c * CHUNK, CHUNK)
+
+    def late_f(c):
+        src = y.at[jnp.where(k == 0, 1, 0), chunk(c)]
+        return remote(src, out_ref.at[chunk(c), pl.ds(0, N)], late_send.at[0, c], late_recv.at[0, c], after)
+
+    def late_b(c):
+        return remote(y.at[1, chunk(c)], out_ref.at[chunk(c), pl.ds(N, N)], late_send.at[1, c], late_recv.at[1, c], before)
+
+    def rows_at(c, i):
+        return pl.ds(c * CHUNK + i * QUARTER, QUARTER)
+
+    def wrap_direct(c, i):
+        at = rows_at(c, i)
+        return remote(y.at[half_mine, at], out_ref.at[at, column_mine], wrap_send.at[c, i], wrap_recv.at[c, i], pair(step))
+
+    def wrap_aside(c, i):
+        at = rows_at(c, i)
+        return remote(y.at[half_mine, at], relay.at[c, i - 1], wrap_send.at[c, i], relay_recv.at[c, i], pair(4 * step))
+
+    def wrap_passed(c, i):
+        dst = out_ref.at[rows_at(c, i), column_mine]
+        return remote(relay.at[c, i - 1], dst, relay_send.at[c, i], wrap_recv.at[c, i], pair(-3 * step))
+
+    def wrap_here(c, i):
+        dst = out_ref.at[rows_at(c, i), column_here]
+        return remote(y.at[half_mine, rows_at(c, i)], dst, wrap_send.at[c, i], wrap_recv.at[c, i], pair(step))
+
+    def rotate(c):
+        moved = mixed(xb[chunk(c), :], mix[...])
+        y[0, chunk(c)] = moved[:, :N]
+        y[1, chunk(c)] = moved[:, N:]
+
+    def send_wraps(c):
+        for i in range(4):
+            if i:
+                pl.when(wraps & (i >= direct_mine))(wrap_aside(c, i).start)
+            if i < 3:
+                pl.when(wraps & (i < direct_mine))(wrap_direct(c, i).start)
+
+    for c in ORDER:
+        if c * CHUNK >= EARLY:
+            rotate(c)
+            send_wraps(c)
+            pl.when(to_after)(late_f(c).start)
+            pl.when(to_before)(late_b(c).start)
+        else:
+
+            @pl.when(edge)
+            def _():
+                rotate(c)
+                send_wraps(c)
 
     keep_left = pltpu.make_async_copy(y.at[0], out_ref.at[:, pl.ds(0, N)], keep.at[0])
     keep_right = pltpu.make_async_copy(y.at[0], out_ref.at[:, pl.ds(N, N)], keep.at[1])
-
-    @pl.when((k == 0) | (k == last))
-    def _():
-        rotate(pl.ds(0, EARLY))
-
     pl.when(k == 0)(keep_left.start)
     pl.when(k == last)(keep_right.start)
+
+    def pass_on(c):
+        for i in range(1, 4):
+
+            @pl.when(edge & (i >= direct_passed))
+            def _():
+                wrap_aside(c, i).wait_recv()
+                wrap_passed(c, i).start()
+
+    def spread(which, first):
+        first.wait_recv()
+        for i in range(1, 8):
+            slot = near.at[which, eighth(seat)]
+            remote(slot, slot, mix_send.at[which, i], mix_recv.at[which, seat], peer(i)[1]).start()
+
+    def early(which):
+        return pltpu.make_async_copy(
+            raw_y.at[which], out_ref.at[pl.ds(0, EARLY), pl.ds(which * N, N)], keep.at[which]
+        )
 
     def finish(which, copies):
         for c in copies:
@@ -321,30 +391,56 @@
             there, device = peer(i)
             slot = near.at[which, eighth(there)]
             remote(slot, slot, mix_send.at[which, i], mix_recv.at[which, there], device).wait_recv()
-        raw_y[which] = mixed(raw[which], near[which])
-        c = pltpu.make_async_copy(raw_y.at[which], out_ref.at[pl.ds(0, EARLY), pl.ds(which * N, N)], keep.at[which])
-        c.start()
+        for c in range(EARLY // CHUNK):
+            raw_y[which, chunk(c)] = mixed(raw[which, chunk(c)], near[which])
+        early(which).start()
+
+    pl.when(to_before)(lambda: spread(0, mix_f))
+    pl.when(to_after)(lambda: spread(1, mix_b))
+    for c in ORDER[:4]:
+        pass_on(c)
+    pl.when(to_before)(lambda: finish(0, raw_f))
+    pl.when(to_after)(lambda: finish(1, raw_b))
+    for c in ORDER[4:]:
+        pass_on(c)
+
+    def sent_mix(which):
         for i in range(1, 8):
             slot = near.at[which, eighth(seat)]
             remote(slot, slot, mix_send.at[which, i], mix_recv.at[which, seat], peer(i)[1]).wait_send()
 
-    pl.when(k > 0)(lambda: finish(0, raw_f))
-    pl.when(k < last)(lambda: finish(1, raw_b))
-
-    for c in [mix_f] + raw_f + late_f:
-        pl.when(k < last)(c.wait_send)
-    for c in [mix_b] + raw_b + late_b:
-        pl.when(k > 0)(c.wait_send)
-    for c in late_f:
-        pl.when(k > 0)(c.wait_recv)
-    for c in late_b:
-        pl.when(k < last)(c.wait_recv)
-    early_left = pltpu.make_async_copy(raw_y.at[0], out_ref.at[pl.ds(0, EARLY), pl.ds(0, N)], keep.at[0])
-    early_right = pltpu.make_async_copy(raw_y.at[1], out_ref.at[pl.ds(0, EARLY), pl.ds(N, N)], keep.at[1])
+    late = [c for c in ORDER if c * CHUNK >= EARLY]
+
+    @pl.when(to_after)
+    def _():
+        for c in [mix_f] + raw_f + [late_f(c) for c in late]:
+            c.wait_send()
+        for c in late:
+            late_b(c).wait_recv()
+        sent_mix(1)
+        early(1).wait()
+
+    @pl.when(to_before)
+    def _():
+        for c in [mix_b] + raw_b + [late_b(c) for c in late]:
+            c.wait_send()
+        for c in late:
+            late_f(c).wait_recv()
+        sent_mix(0)
+        early(0).wait()
+
+    for c in ORDER:
+        for i in range(4):
+
+            @pl.when(wraps)
+            def _():
+                wrap_here(c, i).wait_send()
+                wrap_here(c, i).wait_recv()
+
+            if i:
+                pl.when(edge & (i >= direct_passed))(wrap_passed(c, i).wait_send)
     pl.when(k == 0)(keep_left.wait)
-    pl.when(k > 0)(early_left.wait)
     pl.when(k == last)(keep_right.wait)
-    pl.when(k < last)(early_right.wait)
 
 
 def per_device(matrix):
@@ -362,6 +458,7 @@
             pltpu.VMEM((2, rows, N), f32),
             pltpu.VMEM((2, EARLY, 2 * N), f32),
             pltpu.VMEM((2, EARLY, N), f32),
+            pltpu.VMEM((CHUNKS, 3, QUARTER, N), f32),
             pltpu.VMEM((3 * N, N), f32),
             pltpu.VMEM((4 * q, N), f32),
             pltpu.VMEM((3 * N, N), f32),
@@ -383,8 +480,12 @@
                 dma((2, RAW_PARTS)),
                 dma((2, 8)),
                 dma((2, 8)),
-                dma((2, len(LATE))),
-                dma((2, len(LATE))),
+                dma((2, CHUNKS)),
+                dma((2, CHUNKS)),
+                dma((CHUNKS, 4)),
+                dma((CHUNKS, 4)),
+                dma((CHUNKS, 4)),
+                dma((CHUNKS, 4)),
                 dma((2,)),
             ],
         ],

time: 121 us -> 89.1 us (0.74)
  the two profiles are of different devices: /device:TPU:1 before, /device:TPU:8 now
where the time goes in v3:
time: 89.1 us; the launch traced here: 89 us
  Pallas kernels  86.1 us (97%)
  local copies, waits for them, and re-layouts  2.91 us (3%)
    pallas_call x1, Pallas kernels, per_device(): pl.pallas_call(step_kernel, out_shape=jax.ShapeDtypeStruct(matrix.shape,...  86.1 us
    unnamed x3, local copies, waits for them, and re-layouts  2.91 us

profile of v3, /device:TPU:8, one launch (start us, length us, event | category | flops | bytes accessed | tf_op | source)
XLA Modules:
  0.0 89.0 jit_solution(3698344770763471417)
XLA Ops:
  0.0 0.0 copy-start
  0.0 1.6 %copy-done = f32[2048,256]{1,0:T(8,128)S(1)} copy-done((f32[2048,256]{1,0:T(8,128)S(1)}, f32[2048,256]{1,0:T(8,128)}, u32[]{:S(2)}) %copy-start) | copy-done | bytes 2097176
  1.6 86.1 %jacobi_step.1 = f32[2048,256]{1,0:T(8,128)S(1)} custom-call(f32[2048,256]{1,0:T(8,128)S(1)} %copy-done), custom_call_target="tpu_custom_call" | custom-call | tf_op jit(solution)/shard_map/jacobi_step/pallas_call | solution.py:451
  87.7 1.3 %copy.3 = f32[2048,256]{1,0:T(8,128)} copy(f32[2048,256]{1,0:T(8,128)S(1)} %jacobi_step.1) | data formatting | bytes 4194304
Async XLA Ops:
  0.0 1.6 %copy-start = (f32[2048,256]{1,0:T(8,128)S(1)}, f32[2048,256]{1,0:T(8,128)}, u32[]{:S(2)}) copy-start(f32[2048,256]{1,0:T(8,128)} %x_ref.1) | copy-start | bytes 6291460

commit v4 on v3

--- a/solution.py
+++ b/solution.py
@@ -48,9 +48,14 @@
 
 
 def rounds(gram_ref, out_ref, a_ref, b_ref, g_ref, t_ref, ml_ref, mr_ref):
-    cross = gram_ref[N : 2 * N]
-    a_ref[...] = skew(gram_ref[:N])[:D]
-    b_ref[...] = skew(gram_ref[2 * N :])[:D]
+    cross = gram_ref[:, 0:16, :].reshape(N, N)
+    packed = gram_ref[:, 16:32, :].reshape(N, N)
+    row = lax.broadcasted_iota(jnp.int32, (N, N), 0)
+    column = lax.broadcasted_iota(jnp.int32, (N, N), 1)
+    flipped = packed.T
+    right = jnp.where(row > column, packed, flipped)
+    a_ref[...] = skew(jnp.where(row <= column, packed, flipped))[:D]
+    b_ref[...] = skew(jnp.where(row == column, gram_ref[0, 32:33, :], right))[:D]
     g_ref[pl.ds(N, D), :] = skew(cross.T)[:D]
     t_ref[pl.ds(0, D), :] = skew(cross)[:D]
     ml_ref[...] = jnp.zeros_like(ml_ref)
@@ -123,13 +128,13 @@
 
 
 EARLY = 1024
-RAW_PARTS = 4
-RAW_AT = 2
+RAW_PARTS = 8
+RAW_FIRST = 2
 CHUNK = 256
 CHUNKS = 8
 QUARTER = CHUNK // 4
 ORDER = tuple(range(EARLY // CHUNK, CHUNKS)) + tuple(range(EARLY // CHUNK))
-LOADS = 4
+LOADS = 2
 
 
 def remote(src, dst, send_sem, recv_sem, to):
@@ -166,9 +171,14 @@
         even = even + (cross(high, high) + cross(mid, mid))
         odd = odd + (cross(high, mid) + cross(high, low))
     gram = even + (odd + odd.T)
-    part[:N] = gram[:N, :N]
-    part[N : 2 * N] = gram[:N, N:]
-    part[2 * N :] = gram[N:, N:]
+    row = lax.broadcasted_iota(jnp.int32, (N, N), 0)
+    column = lax.broadcasted_iota(jnp.int32, (N, N), 1)
+    packed = jnp.where(row <= column, gram[:N, :N], gram[N:, N:])
+    diagonal = jnp.sum(jnp.where(row == column, gram[N:, N:], 0.0), axis=0, keepdims=True)
+    for e in range(8):
+        part[e, 0:16] = gram[16 * e : 16 * e + 16, N:]
+        part[e, 16:32] = packed[16 * e : 16 * e + 16]
+        part[e, 32:33] = diagonal if e == 0 else jnp.zeros_like(diagonal)
 
 
 def step_kernel(x_ref, out_ref, xb, y, raw, raw_y, relay, part, half, total, in_core, in_x, in_z, mix, near, round_refs, sems):
@@ -191,7 +201,7 @@
     column_mine = pl.ds(pl.multiple_of(jnp.where(top, 0, N), N), N)
     column_here = pl.ds(pl.multiple_of(jnp.where(top, N, 0), N), N)
     half_mine = jnp.where(top, 0, 1)
-    load, send, recv_core, recv_x, recv_z, recv_gx, recv_gc, raw_send, raw_recv, mix_send, mix_recv, late_send, late_recv, wrap_send, wrap_recv, relay_send, relay_recv, keep = sems
+    load, send, recv_core, recv_x, recv_z, recv_gx, recv_gc, raw_send, raw_recv, mix_send, mix_recv, late_send, late_recv, wrap_send, wrap_recv, relay_send, relay_recv, keep, near_ready, far_ready = sems
 
     def place(z, x, core):
         return {"row": (z * 4 + x) * 2 + core}
@@ -201,20 +211,42 @@
         return other, {"row": z * 8 + other}
 
     barrier = pltpu.get_barrier_semaphore()
-    for i in range(1, 8):
-        pl.semaphore_signal(barrier, inc=1, device_id=peer(i)[1], device_id_type=MESH)
-    for i in range(1, 4):
-        pl.semaphore_signal(barrier, inc=1, device_id=place(lax.rem(z + i, 4), x, core), device_id_type=MESH)
-    for distance in (1, -1, 3, -3, 4, -4):
-        pl.semaphore_signal(barrier, inc=1, device_id=pair(distance), device_id_type=MESH)
+
+    def chip(distance, core):
+        return {"pair": lax.rem(k + distance + last + 1, last + 1), "row": (z * 4 + x) * 2 + core}
+
+    def exists(distance):
+        return (k + distance >= 0) & (k + distance <= last)
+
+    pairs = [
+        (1, exists(1)), (-1, exists(-1)), (4, edge & exists(4)), (-4, edge & exists(-4)), (3, pz == 0), (-3, top),
+    ]
+    hears = 7
+    for distance, there in pairs:
+        hears = hears + 2 * there.astype(jnp.int32)
+
+    def call(to):
+        pl.semaphore_signal(barrier, inc=1, device_id=to, device_id_type=MESH)
+
+    pl.when(core == 1)(lambda: call(place(z, x, 0)))
+    for i in range(1, 4):
+        call(place(lax.rem(z + i, 4), x, 1))
+    for i in range(1, 4):
+        call(place(z, lax.rem(x + i, 4), 0))
+    for distance, there in pairs:
+        pl.when(there)(lambda: call(chip(distance, 0)))
 
     partial_gram(x_ref, xb, part, load)
-    pl.semaphore_wait(barrier, 16)
-
-    h = 3 * N // 2
-    q = h // 4
-    mine = pl.ds(pl.multiple_of(core * h, 8), h)
-    other = pl.ds(pl.multiple_of((1 - core) * h, 8), h)
+
+    @pl.when(core == 0)
+    def _():
+        pl.semaphore_wait(barrier, hears)
+        pl.semaphore_signal(near_ready, inc=1, device_id=place(z, x, 1), device_id_type=MESH)
+
+    pl.when(core == 1)(lambda: pl.semaphore_wait(near_ready, 1))
+
+    mine = pl.ds(core * 4, 4)
+    other = pl.ds((1 - core) * 4, 4)
     sent = []
     c = remote(part.at[other], in_core, send.at[0], recv_core, place(z, x, 1 - core))
     c.start()
@@ -227,43 +259,44 @@
         raw_f.append(remote(xb.at[at], raw.at[0, at], raw_send.at[0, j], raw_recv.at[0, j], after))
         raw_b.append(remote(xb.at[at], raw.at[1, at], raw_send.at[1, j], raw_recv.at[1, j], before))
 
-    def start_raw():
-        for j in range(RAW_PARTS):
+    def start_raw(begin, end):
+        for j in range(begin, end):
             pl.when(to_after)(raw_f[j].start)
             pl.when(to_before)(raw_b[j].start)
 
-    if RAW_AT == 0:
-        start_raw()
+    start_raw(0, RAW_FIRST)
     c.wait_recv()
     half[...] = part[mine] + in_core[...]
 
-    quarter = pl.ds(pl.multiple_of(x * q, 8), q)
     for i in range(1, 4):
         xt = lax.rem(x + i, 4)
-        c = remote(half.at[pl.ds(pl.multiple_of(xt * q, 8), q)], in_x.at[x], send.at[i], recv_x.at[x], place(z, xt, core))
+        c = remote(half.at[xt], in_x.at[x], send.at[i], recv_x.at[x], place(z, xt, core))
         c.start()
         sent.append(c)
-    in_x[x] = half[quarter]
+    in_x[x] = half[x]
     for i in range(1, 4):
         xf = lax.rem(x + i, 4)
         remote(in_x.at[xf], in_x.at[xf], send.at[i], recv_x.at[xf], place(z, xf, core)).wait_recv()
     in_z[z] = (in_x[0] + in_x[1]) + (in_x[2] + in_x[3])
 
+    @pl.when(core == 1)
+    def _():
+        pl.semaphore_wait(barrier, 6)
+        pl.semaphore_signal(far_ready, inc=1, device_id=place(z, x, 0), device_id_type=MESH)
+
+    pl.when(core == 0)(lambda: pl.semaphore_wait(far_ready, 1))
     for i in range(1, 4):
         zt = lax.rem(z + i, 4)
         c = remote(in_z.at[z], in_z.at[z], send.at[3 + i], recv_z.at[z], place(zt, x, core))
         c.start()
         sent.append(c)
-    if RAW_AT == 1:
-        start_raw()
     for i in range(1, 4):
         zf = lax.rem(z + i, 4)
         remote(in_z.at[zf], in_z.at[zf], send.at[3 + i], recv_z.at[zf], place(zf, x, core)).wait_recv()
-    if RAW_AT == 2:
-        start_raw()
+    start_raw(RAW_FIRST, RAW_PARTS)
 
     def rows_of(core, x):
-        return total.at[pl.ds(pl.multiple_of(core * h + x * q, 8), q)]
+        return total.at[core * 4 + x]
 
     own = rows_of(core, x)
     own[...] = (in_z[0] + in_z[1]) + (in_z[2] + in_z[3])
@@ -445,13 +478,13 @@
 
 def per_device(matrix):
     rows = matrix.shape[0]
-    q = 3 * N // 8
+    eighth = (33, N)
     dma = pltpu.SemaphoreType.DMA
     f32 = jnp.float32
     return pl.pallas_call(
         step_kernel,
         out_shape=jax.ShapeDtypeStruct(matrix.shape, f32),
-        in_specs=[pl.BlockSpec(memory_space=pl.ANY)],
+        in_specs=[pl.BlockSpec(memory_space=pltpu.HBM)],
         out_specs=pl.BlockSpec(memory_space=pl.ANY),
         scratch_shapes=[
             pltpu.VMEM((rows, 2 * N), f32),
@@ -459,12 +492,12 @@
             pltpu.VMEM((2, EARLY, 2 * N), f32),
             pltpu.VMEM((2, EARLY, N), f32),
             pltpu.VMEM((CHUNKS, 3, QUARTER, N), f32),
-            pltpu.VMEM((3 * N, N), f32),
-            pltpu.VMEM((4 * q, N), f32),
-            pltpu.VMEM((3 * N, N), f32),
-            pltpu.VMEM((4 * q, N), f32),
-            pltpu.VMEM((4, q, N), f32),
-            pltpu.VMEM((4, q, N), f32),
+            pltpu.VMEM((8, *eighth), f32),
+            pltpu.VMEM((4, *eighth), f32),
+            pltpu.VMEM((8, *eighth), f32),
+            pltpu.VMEM((4, *eighth), f32),
+            pltpu.VMEM((4, *eighth), f32),
+            pltpu.VMEM((4, *eighth), f32),
             pltpu.VMEM((2 * N, 2 * N), f32),
             pltpu.VMEM((2, N, 2 * N), f32),
             ROUND_SCRATCH,
@@ -487,6 +520,8 @@
                 dma((CHUNKS, 4)),
                 dma((CHUNKS, 4)),
                 dma((2,)),
+                pltpu.SemaphoreType.REGULAR,
+                pltpu.SemaphoreType.REGULAR,
             ],
         ],
         compiler_params=pltpu.CompilerParams(collective_id=0, has_side_effects=True, vmem_limit_bytes=48 << 20),

time: 89.1 us -> 89.9 us (level)
  no operation moved by 1% of the time
where the time goes in v4:
time: 89.9 us; the launch traced here: 89.8 us
  Pallas kernels  86.9 us (97%)
  local copies, waits for them, and re-layouts  2.91 us (3%)
    pallas_call x1, Pallas kernels, per_device(): pl.pallas_call(step_kernel, out_shape=jax.ShapeDtypeStruct(matrix.shape,...  86.9 us
    unnamed x3, local copies, waits for them, and re-layouts  2.91 us

profile of v4, /device:TPU:8, one launch (start us, length us, event | category | flops | bytes accessed | tf_op | source)
XLA Modules:
  0.0 89.8 jit_solution(650582461413824101)
XLA Ops:
  0.0 0.0 copy-start
  0.0 1.6 %copy-done = f32[2048,256]{1,0:T(8,128)S(1)} copy-done((f32[2048,256]{1,0:T(8,128)S(1)}, f32[2048,256]{1,0:T(8,128)}, u32[]{:S(2)}) %copy-start) | copy-done | bytes 2097176
  1.6 86.9 %jacobi_step.1 = f32[2048,256]{1,0:T(8,128)S(1)} custom-call(f32[2048,256]{1,0:T(8,128)S(1)} %copy-done), custom_call_target="tpu_custom_call" | custom-call | tf_op jit(solution)/shard_map/jacobi_step/pallas_call | solution.py:484
  88.5 1.3 %copy.3 = f32[2048,256]{1,0:T(8,128)} copy(f32[2048,256]{1,0:T(8,128)S(1)} %jacobi_step.1) | data formatting | bytes 4194304
Async XLA Ops:
  0.0 1.6 %copy-start = (f32[2048,256]{1,0:T(8,128)S(1)}, f32[2048,256]{1,0:T(8,128)}, u32[]{:S(2)}) copy-start(f32[2048,256]{1,0:T(8,128)} %x_ref.1) | copy-start | bytes 6291460

commit v5 on v4

--- a/solution.py
+++ b/solution.py
@@ -9,8 +9,8 @@
 
 N = 128
 D = 72
-STAGES = 8
-UNROLL = 8
+STAGES = 4
+UNROLL = 16
 MESH = pl.DeviceIdType.MESH
 HIGH = lax.Precision.HIGHEST
 
@@ -66,32 +66,25 @@
     def back(x, lanes):
         return pltpu.roll(x, N - lanes, 1)
 
-    def one_round(rows, r, carry):
-        da, db, dg, ea, eb, eg, a1, t1, g1, b1 = carry
-        c, s = angles(da, db, dg)
-        ce, se = back(c, 1), back(s, 1)
-        na = c * (c * da - s * dg) - s * (c * dg - s * db)
-        nb = se * (se * ea + ce * eg) + ce * (se * eg + ce * eb)
-        ng = c * (se * a1 + ce * t1) - s * (se * g1 + ce * b1)
+    def turned(a, t, g, b, c, s, cc, ss):
+        a, t = c * a - s * t, s * a + c * t
+        g, b = c * g - s * b, s * g + c * b
+        a, g = cc * a - ss * g, ss * a + cc * g
+        t, b = cc * t - ss * b, ss * t + cc * b
+        return a, t, g, b
+
+    def full_round(rows, r, c, s):
         n = max(rows, D)
         cd = fan(jnp.broadcast_to(c, (n, N)))
         sd = fan(jnp.broadcast_to(s, (n, N)))
-        a, b = a_ref[...], b_ref[...]
         gw, tw = pl.ds(N - r, D), pl.ds(r, D)
-        g, t = g_ref[gw, :], t_ref[tw, :]
-        a, t = c * a - s * t, s * a + c * t
-        g, b = c * g - s * b, s * g + c * b
-        ch, sh = cd[:D], sd[:D]
-        a, g = ch * a - sh * g, sh * a + ch * g
-        t, b = ch * t - sh * b, sh * t + ch * b
-        ahead = (back(na, 1), back(nb, 1), back(ng, 1), back(a[1:2], 1), back(t[2:3], 2), back(g[0:1], 1), back(b[1:2], 2))
-        b = back(b, 1)
-        t = back(t, 1)
+        a, t, g, b = turned(a_ref[...], t_ref[tw, :], g_ref[gw, :], b_ref[...], c, s, cd[:D], sd[:D])
+        b_next, t_next = back(b, 1), back(t, 1)
         a_ref[...] = a
-        b_ref[...] = b
+        b_ref[...] = b_next
         g_ref[gw, :] = g
-        t_ref[tw, :] = t
-        g_ref[pl.ds(N - 1 - r, 1), :] = t[1:2]
+        t_ref[tw, :] = t_next
+        g_ref[pl.ds(N - 1 - r, 1), :] = t_next[1:2]
         t_ref[pl.ds(r + D, 1), :] = back(g[N - D : N - D + 1], N - D + 1)
         mw = pl.ds(N - r, rows)
         cm, sm = cd[:rows], sd[:rows]
@@ -99,15 +92,51 @@
             left, right = ml_ref[h, pl.ds(0, rows), :], mr_ref[h, mw, :]
             ml_ref[h, pl.ds(0, rows), :] = cm * left - sm * right
             mr_ref[h, mw, :] = sm * left + cm * right
-        return (na, nb, ng) + ahead
+        return a, t, g, b
+
+    def two_rounds(rows, r, carry):
+        (a0, b0, g0), (a1, b1, g1), (a2, b2, g2), near, middle, far = carry
+        c0, s0 = angles(a0, b0, g0)
+        c1, s1, c2, s2 = back(c0, 1), back(s0, 1), back(c0, 2), back(s0, 2)
+        diag0 = turned(a0, g0, g0, b0, c0, s0, c0, s0)
+        diag1 = turned(a1, g1, g1, b1, c1, s1, c1, s1)
+        diag2 = turned(a2, g2, g2, b2, c2, s2, c2, s2)
+        near = turned(*near, c1, s1, c0, s0)
+        middle = turned(*middle, c2, s2, c1, s1)
+        far = turned(*far, c2, s2, c0, s0)
+        full_round(rows, r, c0, s0)
+        cross = diag1[2]
+        a0, b0, g0 = diag0[0], diag1[3], near[1]
+        a1, b1, g1 = diag1[0], diag2[3], middle[1]
+        c0, s0 = angles(a0, b0, g0)
+        c1, s1 = angles(a1, b1, g1)
+        diag0 = turned(a0, g0, g0, b0, c0, s0, c0, s0)
+        diag1 = turned(a1, g1, g1, b1, c1, s1, c1, s1)
+        near = turned(near[0], far[1], cross, middle[3], c1, s1, c0, s0)
+        a, t, g, b = full_round(rows, r + 1, c0, s0)
+        first = (diag0[0], diag1[3], near[1])
+        return (
+            first,
+            tuple(back(v, 1) for v in first),
+            tuple(back(v, 2) for v in first),
+            (back(a[1:2], 1), back(t[2:3], 2), back(g[0:1], 1), back(b[1:2], 2)),
+            (back(a[1:2], 2), back(t[2:3], 3), back(g[0:1], 2), back(b[1:2], 3)),
+            (back(a[2:3], 2), back(t[3:4], 3), back(g[1:2], 2), back(b[2:3], 3)),
+        )
 
     def group(rows, i, carry):
-        for u in range(UNROLL):
-            carry = one_round(rows, UNROLL * i + u, carry)
+        for u in range(0, UNROLL, 2):
+            carry = two_rounds(rows, UNROLL * i + u, carry)
         return carry
 
+    def entries(d, lanes):
+        rows = (a_ref[d : d + 1, :], t_ref[d : d + 1, :], g_ref[N + d : N + d + 1, :], b_ref[d : d + 1, :])
+        return tuple(back(v, lanes) for v in rows)
+
     first = (a_ref[0:1, :], b_ref[0:1, :], t_ref[0:1, :])
-    carry = first + tuple(back(v, 1) for v in first + (a_ref[1:2, :], t_ref[1:2, :], g_ref[N + 1 : N + 2, :], b_ref[1:2, :]))
+    carry = (
+        first, tuple(back(v, 1) for v in first), tuple(back(v, 2) for v in first), entries(1, 1), entries(1, 2), entries(2, 2)
+    )
     for stage in range(STAGES):
         begin, end = N * stage // STAGES, N * (stage + 1) // STAGES
         carry = lax.fori_loop(begin // UNROLL, end // UNROLL, functools.partial(group, end), carry)
@@ -129,7 +158,7 @@
 
 EARLY = 1024
 RAW_PARTS = 8
-RAW_FIRST = 2
+RAW_FIRST = 0
 CHUNK = 256
 CHUNKS = 8
 QUARTER = CHUNK // 4
@@ -373,17 +402,14 @@
         y[0, chunk(c)] = moved[:, :N]
         y[1, chunk(c)] = moved[:, N:]
 
-    def send_wraps(c):
-        for i in range(4):
-            if i:
-                pl.when(wraps & (i >= direct_mine))(wrap_aside(c, i).start)
-            if i < 3:
-                pl.when(wraps & (i < direct_mine))(wrap_direct(c, i).start)
+    def send_aside(c):
+        for i in range(1, 4):
+            pl.when(wraps & (i >= direct_mine))(wrap_aside(c, i).start)
 
     for c in ORDER:
         if c * CHUNK >= EARLY:
             rotate(c)
-            send_wraps(c)
+            send_aside(c)
             pl.when(to_after)(late_f(c).start)
             pl.when(to_before)(late_b(c).start)
         else:
@@ -391,7 +417,11 @@
             @pl.when(edge)
             def _():
                 rotate(c)
-                send_wraps(c)
+                send_aside(c)
+
+    for c in ORDER:
+        for i in range(3):
+            pl.when(wraps & (i < direct_mine))(wrap_direct(c, i).start)
 
     keep_left = pltpu.make_async_copy(y.at[0], out_ref.at[:, pl.ds(0, N)], keep.at[0])
     keep_right = pltpu.make_async_copy(y.at[0], out_ref.at[:, pl.ds(N, N)], keep.at[1])
@@ -430,12 +460,10 @@
 
     pl.when(to_before)(lambda: spread(0, mix_f))
     pl.when(to_after)(lambda: spread(1, mix_b))
-    for c in ORDER[:4]:
+    for c in ORDER:
         pass_on(c)
     pl.when(to_before)(lambda: finish(0, raw_f))
     pl.when(to_after)(lambda: finish(1, raw_b))
-    for c in ORDER[4:]:
-        pass_on(c)
 
     def sent_mix(which):
         for i in range(1, 8):

time: 89.9 us -> 83.7 us (0.931)
  Pallas kernels: 86.9 us -> 80.6 us
    pallas_call x1, Pallas kernels: 86.9 us -> 80.6 us  [per_device(): pl.pallas_call(step_kernel, out_shape=jax.ShapeDtypeStruct(matrix.shape,...]
where the time goes in v5:
time: 83.7 us; the launch traced here: 83.5 us
  Pallas kernels  80.6 us (96%)
  local copies, waits for them, and re-layouts  2.91 us (3%)
    pallas_call x1, Pallas kernels, per_device(): pl.pallas_call(step_kernel, out_shape=jax.ShapeDtypeStruct(matrix.shape,...  80.6 us
    unnamed x3, local copies, waits for them, and re-layouts  2.91 us

profile of v5, /device:TPU:8, one launch (start us, length us, event | category | flops | bytes accessed | tf_op | source)
XLA Modules:
  0.0 83.5 jit_solution(10377526882450287523)
XLA Ops:
  0.0 0.0 copy-start
  0.0 1.6 %copy-done = f32[2048,256]{1,0:T(8,128)S(1)} copy-done((f32[2048,256]{1,0:T(8,128)S(1)}, f32[2048,256]{1,0:T(8,128)}, u32[]{:S(2)}) %copy-start) | copy-done | bytes 2097176
  1.6 80.6 %jacobi_step.1 = f32[2048,256]{1,0:T(8,128)S(1)} custom-call(f32[2048,256]{1,0:T(8,128)S(1)} %copy-done), custom_call_target="tpu_custom_call" | custom-call | tf_op jit(solution)/shard_map/jacobi_step/pallas_call | solution.py:512
  82.2 1.3 %copy.3 = f32[2048,256]{1,0:T(8,128)} copy(f32[2048,256]{1,0:T(8,128)S(1)} %jacobi_step.1) | data formatting | bytes 4194304
Async XLA Ops:
  0.0 1.6 %copy-start = (f32[2048,256]{1,0:T(8,128)S(1)}, f32[2048,256]{1,0:T(8,128)}, u32[]{:S(2)}) copy-start(f32[2048,256]{1,0:T(8,128)} %x_ref.1) | copy-start | bytes 6291460

commit v6 on v5

--- a/solution.py
+++ b/solution.py
@@ -9,7 +9,7 @@
 
 N = 128
 D = 72
-STAGES = 4
+STAGES = 8
 UNROLL = 16
 MESH = pl.DeviceIdType.MESH
 HIGH = lax.Precision.HIGHEST
@@ -322,7 +322,6 @@
     for i in range(1, 4):
         zf = lax.rem(z + i, 4)
         remote(in_z.at[zf], in_z.at[zf], send.at[3 + i], recv_z.at[zf], place(zf, x, core)).wait_recv()
-    start_raw(RAW_FIRST, RAW_PARTS)
 
     def rows_of(core, x):
         return total.at[core * 4 + x]
@@ -333,6 +332,7 @@
         c = remote(own, own, send.at[6 + i], recv_gx.at[x], place(z, lax.rem(x + i, 4), core))
         c.start()
         sent.append(c)
+    start_raw(RAW_FIRST, RAW_PARTS)
     for i in range(4):
         xf = lax.rem(x + i, 4)
         there = rows_of(core, xf)

time: 83.7 us -> 83.1 us (level)
  no operation moved by 1% of the time
where the time goes in v6:
time: 83.1 us; the launch traced here: 82.9 us
  Pallas kernels  80 us (96%)
  local copies, waits for them, and re-layouts  2.91 us (4%)
    pallas_call x1, Pallas kernels, per_device(): pl.pallas_call(step_kernel, out_shape=jax.ShapeDtypeStruct(matrix.shape,...  80 us
    unnamed x3, local copies, waits for them, and re-layouts  2.91 us

profile of v6, /device:TPU:8, one launch (start us, length us, event | category | flops | bytes accessed | tf_op | source)
XLA Modules:
  0.0 82.9 jit_solution(1690482990770230628)
XLA Ops:
  0.0 0.0 copy-start
  0.0 1.6 %copy-done = f32[2048,256]{1,0:T(8,128)S(1)} copy-done((f32[2048,256]{1,0:T(8,128)S(1)}, f32[2048,256]{1,0:T(8,128)}, u32[]{:S(2)}) %copy-start) | copy-done | bytes 2097176
  1.6 80.0 %jacobi_step.1 = f32[2048,256]{1,0:T(8,128)S(1)} custom-call(f32[2048,256]{1,0:T(8,128)S(1)} %copy-done), custom_call_target="tpu_custom_call" | custom-call | tf_op jit(solution)/shard_map/jacobi_step/pallas_call | solution.py:512
  81.6 1.3 %copy.3 = f32[2048,256]{1,0:T(8,128)} copy(f32[2048,256]{1,0:T(8,128)S(1)} %jacobi_step.1) | data formatting | bytes 4194304
Async XLA Ops:
  0.0 1.6 %copy-start = (f32[2048,256]{1,0:T(8,128)S(1)}, f32[2048,256]{1,0:T(8,128)}, u32[]{:S(2)}) copy-start(f32[2048,256]{1,0:T(8,128)} %x_ref.1) | copy-start | bytes 6291460

commit v7 on v6

--- a/solution.py
+++ b/solution.py
@@ -345,10 +345,9 @@
         xf = lax.rem(x + i, 4)
         there = rows_of(1 - core, xf)
         remote(there, there, send.at[10 + i], recv_gc.at[xf], place(z, x, 1 - core)).wait_recv()
+    rounds(total, mix, *round_refs)
     for c in sent:
         c.wait_send()
-
-    rounds(total, mix, *round_refs)
 
     seat = lax.rem(me, 8)
     share = N // 8

time: 83.1 us -> 83.1 us (level)
  no operation moved by 1% of the time
where the time goes in v7:
time: 83.1 us; the launch traced here: 82.9 us
  Pallas kernels  80 us (96%)
  local copies, waits for them, and re-layouts  2.91 us (4%)
    pallas_call x1, Pallas kernels, per_device(): pl.pallas_call(step_kernel, out_shape=jax.ShapeDtypeStruct(matrix.shape,...  80 us
    unnamed x3, local copies, waits for them, and re-layouts  2.91 us

profile of v7, /device:TPU:8, one launch (start us, length us, event | category | flops | bytes accessed | tf_op | source)
XLA Modules:
  0.0 82.9 jit_solution(3851580685824389412)
XLA Ops:
  0.0 0.0 copy-start
  0.0 1.6 %copy-done = f32[2048,256]{1,0:T(8,128)S(1)} copy-done((f32[2048,256]{1,0:T(8,128)S(1)}, f32[2048,256]{1,0:T(8,128)}, u32[]{:S(2)}) %copy-start) | copy-done | bytes 2097176
  1.6 80.0 %jacobi_step.1 = f32[2048,256]{1,0:T(8,128)S(1)} custom-call(f32[2048,256]{1,0:T(8,128)S(1)} %copy-done), custom_call_target="tpu_custom_call" | custom-call | tf_op jit(solution)/shard_map/jacobi_step/pallas_call | solution.py:511
  81.6 1.3 %copy.3 = f32[2048,256]{1,0:T(8,128)} copy(f32[2048,256]{1,0:T(8,128)S(1)} %jacobi_step.1) | data formatting | bytes 4194304
Async XLA Ops:
  0.0 1.6 %copy-start = (f32[2048,256]{1,0:T(8,128)S(1)}, f32[2048,256]{1,0:T(8,128)}, u32[]{:S(2)}) copy-start(f32[2048,256]{1,0:T(8,128)} %x_ref.1) | copy-start | bytes 6291460
